TPU v7x, 128 devices: a whole 4x4x4 slice. The times are simulated.
128 devices in a mesh: fsdp: 32 (over x, y, core), adapter: 4 (over z).
Axes of the slice: x: 4, y: 4, z: 4, core: 2. Of those that a mesh axis runs over, the one named last changes fastest.
Arguments:
- hidden: bfloat16 [16384, 14336], P('fsdp', 'adapter'), may hold values from -6 to 6
- down_weight: bfloat16 [14336, 4096], P('adapter', 'fsdp'), may hold values from -0.046875 to 0.046875
- tile_adapter_choice: int32 [128, 1], P('fsdp'), may hold values from 0 to 3; in each aligned block of 4 rows (0 to 3, 4 to 7, ...) at most 2 rows name the same one
- adapter_ranks: int32 [128], P('fsdp'), may hold values from 16 to 256, as said below
- adapter_down_matrices: bfloat16 [128, 14336, 256], P(('fsdp', 'adapter')), may hold values from -0.046875 to 0.046875
- adapter_up_matrices: bfloat16 [128, 4096, 256], P(('fsdp', 'adapter')), may hold values from -0.375 to 0.375
Outputs:
- adapted: bfloat16 [16384, 4096], P('fsdp', 'adapter')
Inputs may be any that keep to these rules, and one draw needn't show every extreme that they name: `tile_adapter_choice`: adapter k of fsdp index g is global adapter g * 4 + k; among the 4 tiles of one fsdp index no adapter is named by more than 2 tiles. `adapter_ranks`: multiples of 16; some adapter has rank 256.
All inputs are finite; a program needn't handle non-finite values.
Results may differ from a plain program's by a relative error of at most 0.015.
Values may be sent and summed in bfloat16 or wider, within the bound.
A program may use at most 128 MiB of HBM per device.

v0:
```python
import jax
import jax.numpy as jnp
from jax import lax
from jax.sharding import PartitionSpec as P

TILE_ROWS = 128
CAP = 2


adapter_alpha = 32.0


def make_dispatch(tile_ids, owners):
    matches = (tile_ids[:, None] == jnp.arange(owners)[None, :]).astype(jnp.int32)
    slot_index = jnp.sum(jnp.cumsum(matches, axis=0) * matches, axis=1) - 1
    return (
        (tile_ids[:, None, None] == jnp.arange(owners)[None, :, None])
        & (slot_index[:, None, None] == jnp.arange(CAP)[None, None, :])
    ).astype(jnp.bfloat16)


def holder_delta(
    arrived_rows, adapter_down_matrices, adapter_up_matrices, rank_valid_mask, holder_scale
):
    slot_positions = arrived_rows.shape[1]
    flattened_rows = arrived_rows.reshape(slot_positions * TILE_ROWS, arrived_rows.shape[3])
    rank_product = jnp.dot(
        flattened_rows, adapter_down_matrices[0], preferred_element_type=jnp.float32
    )
    rank_product = jnp.where(rank_valid_mask[None, :], rank_product, 0.0).astype(jnp.bfloat16)
    complete_delta = (
        lax.dot_general(
            rank_product,
            adapter_up_matrices[0],
            (((1,), (1,)), ((), ())),
            preferred_element_type=jnp.float32,
        )
        * holder_scale
    )
    return complete_delta.astype(jnp.bfloat16).reshape(
        1, slot_positions, TILE_ROWS, adapter_up_matrices.shape[1]
    )


def on_device(
    hidden,
    down_weight,
    tile_adapter_choice,
    adapter_ranks,
    adapter_down_matrices,
    adapter_up_matrices,
):
    owners = lax.axis_size("adapter")
    tok_rows = hidden.shape[0]
    unit_part = hidden.shape[1]
    tile_count = tok_rows // TILE_ROWS
    rank_span_width = adapter_down_matrices.shape[2]
    partial_value = jnp.dot(
        hidden,
        lax.all_gather(down_weight, "fsdp", axis=1, tiled=True),
        preferred_element_type=jnp.float32,
    )
    rounded = lax.optimization_barrier(partial_value.astype(jnp.bfloat16)).astype(jnp.float32)
    tile_ids = tile_adapter_choice[:, 0]
    blocks = hidden.reshape(tile_count, TILE_ROWS, unit_part)
    own_index = lax.axis_index("adapter")
    holder_rank = jnp.sum(jnp.where(jnp.arange(owners) == own_index, adapter_ranks, 0))
    holder_scale = adapter_alpha / holder_rank.astype(jnp.float32)
    rank_valid_mask = jnp.arange(rank_span_width) < holder_rank
    base_out = lax.psum_scatter(
        rounded.astype(jnp.bfloat16), "adapter", scatter_dimension=1, tiled=True
    ).astype(jnp.float32)
    dispatch = make_dispatch(tile_ids, owners)
    outgoing = jnp.einsum(
        "toc,tpf->ocpf", dispatch, blocks, preferred_element_type=jnp.float32
    ).astype(jnp.bfloat16)
    complete_delta = holder_delta(
        lax.all_to_all(outgoing, "adapter", split_axis=0, concat_axis=3, tiled=True),
        adapter_down_matrices,
        adapter_up_matrices,
        rank_valid_mask,
        holder_scale,
    )
    returned = lax.all_to_all(complete_delta, "adapter", split_axis=3, concat_axis=0, tiled=True)
    delta = jnp.einsum("toc,ocpd->tpd", dispatch, returned, preferred_element_type=jnp.float32)
    adapted = base_out + delta.reshape(tok_rows, base_out.shape[1])
    return adapted.astype(jnp.bfloat16)


def solution(mesh):
    return jax.shard_map(
        on_device,
        mesh=mesh,
        in_specs=(
            P("fsdp", "adapter"),
            P("adapter", "fsdp"),
            P("fsdp", None),
            P("fsdp"),
            P(("fsdp", "adapter"), None, None),
            P(("fsdp", "adapter"), None, None),
        ),
        out_specs=P("fsdp", "adapter"),
        check_vma=False,
    )
```

profile of v0, /device:TPU:39, one launch (start us, length us, event | category | flops | bytes accessed | tf_op | source)
XLA Modules:
  0.0 362.3 jit_solution(9060826556743008275)
XLA Ops:
  6.5 0.0 copy-start
  6.5 0.0 all-gather.2.cloned.1.call-start
  6.5 0.7 all-gather.2.cloned.1.call-update
  7.3 0.0 reduce-scatter.2.cloned.1.call-start
  7.3 0.7 iota_compare_fusion
  8.1 0.8 select_reduce_fusion
  8.9 117.4 %all-gather.2.cloned.1.call-done = bf16[3584,4096]{1,0:T(8,128)(2,1)} async-done(((bf16[3584,128]{1,0:T(8,128)(2,1)}), bf16[3584,4096]{1,0:T(8,128)(2,1)}) %all-gather.2.cloned.1.call-update) | async-done | bytes 29360144 | tf_op jit(solution)/shard_map/all_gather | solution.py:60
  126.3 23.0 %convolution_convert_fusion.1 = bf16[512,4096]{1,0:T(8,128)(2,1)} fusion(bf16[512,3584]{1,0:T(8,128)(2,1)} %param.6, bf16[3584,4096]{1,0:T(8,128)(2,1)} %all-gather.2.cloned.1.call-done), kind=kOutput, calls=%fused_computation.3 | convolution fusion | flops 15034482688 | bytes 37224448 | tf_op jit(solution)/shard_map/dot_general | solution.py:58
  149.3 0.0 reduce-scatter.2.cloned.1.call-update
  149.3 7.1 %convolution_convert_fusion = bf16[4,2,128,3584]{3,0,2,1:T(4,128)(2,1)S(1)} fusion(bf16[4,128,3584]{2,1,0:T(8,128)(2,1)} %bitcast.53, pred[4,2]{0,1:T(4,128)(4,1)S(1)} %iota_compare_fusion.2, pred[4,4]{1,0:T(4,128)(4,1)S(1)} %get-tuple-element.5), kind=kOutput, calls=%fused_computation | convolution fusion | flops 33030176 | bytes 11010072 | tf_op jit(solution)/shard_map/toc,tpf->ocpf/dot_general | solution.py:74
  156.4 4.6 %copy.19 = bf16[4,2,128,3584]{3,2,1,0:T(8,128)(2,1)} copy(bf16[4,2,128,3584]{3,0,2,1:T(4,128)(2,1)S(1)} %convolution_convert_fusion) | data formatting | bytes 14680064 | tf_op jit(solution)/shard_map/convert_element_type | solution.py:76
  161.0 0.0 copy-start.1
  161.0 5.7 %all-to-all-start = ((bf16[4,2,128,3584]{3,2,1,0:T(8,128)(2,1)}), bf16[4,2,128,3584]{3,2,1,0:T(8,128)(2,1)}, u32[]{:S(2)}, u32[]{:S(2)}) async-start(bf16[4,2,128,3584]{3,2,1,0:T(8,128)(2,1)} %copy.19), calls=%async_computation.1 | async-start | bytes 14680064 | tf_op jit(solution)/shard_map/all_to_all | solution.py:78
  166.8 0.0 copy-done.1
  166.8 0.6 fusion.26
  168.1 0.7 iota_compare_fusion.1
  168.7 105.1 %all-to-all-done = bf16[4,2,128,3584]{3,2,1,0:T(8,128)(2,1)} async-done(((bf16[4,2,128,3584]{3,2,1,0:T(8,128)(2,1)}), bf16[4,2,128,3584]{3,2,1,0:T(8,128)(2,1)}, u32[]{:S(2)}, u32[]{:S(2)}) %all-to-all-start) | async-done | bytes 7340064 | tf_op jit(solution)/shard_map/all_to_all | solution.py:78
  273.9 11.8 %copy.20 = bf16[1,2,128,4,3584]{4,3,2,1,0:T(4,128)(2,1)} copy(bf16[1,2,128,4,3584]{4,2,1,3,0:T(8,128)(2,1)} %bitcast.6) | data formatting | bytes 14680064 | tf_op jit(solution)/shard_map/all_to_all | solution.py:78
  285.7 7.9 %copy.29 = bf16[32,8,4,3584]{3,1,2,0:T(8,128)(2,1)} copy(bf16[32,8,4,3584]{3,2,1,0:T(4,128)(2,1)} %bitcast.50) | data formatting | bytes 14680064
  293.6 0.0 copy-done
  293.6 10.3 %fusion.2 = bf16[256,4096]{1,0:T(8,128)(2,1)} fusion(bf16[1,4096,256]{2,1,0:T(8,128)(2,1)S(1)} %copy-done, f32[]{:T(128)S(6)} %div.3, bf16[256,14336]{1,0:T(8,128)(2,1)} %bitcast.52, bf16[1,14336,256]{2,1,0:T(8,128)(2,1)} %param.10, pred[256]{0:T(512)(128)(4,1)S(1)} %iota_compare_fusion.1), kind=kOutput, calls=%fused_computation.5 | convolution fusion | flops 2418147328 | bytes 18874628 | tf_op jit(solution)/shard_map/dot_general | solution.py:32
  303.9 6.2 %copy.21 = bf16[1,2,128,4096]{2,1,0,3:T(2,128)(2,1)} copy(bf16[1,2,128,4096]{3,2,1,0:T(8,128)(2,1)} %bitcast.54) | data formatting | bytes 4194304 | tf_op jit(solution)/shard_map/reshape | solution.py:40
  310.0 29.8 %all_to_all.33 = bf16[1,2,128,4096]{2,1,0,3:T(2,128)(2,1)} all-to-all(bf16[1,2,128,4096]{2,1,0,3:T(2,128)(2,1)} %copy.21), channel_id=1, replica_groups=mesh['fsdp'=32,'adapter'=4] {'adapter'}, dimensions={3} | all-to-all | bytes 4194304 | tf_op jit(solution)/shard_map/all_to_all | solution.py:84
  339.9 6.5 %copy.28 = bf16[1,2,128,4,1024]{4,3,1,2,0:T(4,128)(2,1)} copy(bf16[1,2,128,4,1024]{2,1,4,3,0:T(2,128)(2,1)} %bitcast.51) | data formatting | bytes 4194304 | tf_op jit(solution)/shard_map/all_to_all | solution.py:84
  346.4 3.3 fusion.9
  349.7 2.6 copy.23
  352.3 0.0 reduce-scatter.2.cloned.1.call-done
  352.3 3.2 fusion.7
  (3 shorter events, 0.1 us)
Async XLA Ops:
  6.5 287.0 %copy-start = (bf16[1,4096,256]{2,1,0:T(8,128)(2,1)S(1)}, bf16[1,4096,256]{2,1,0:T(8,128)(2,1)}, u32[]{:S(2)}) copy-start(bf16[1,4096,256]{2,1,0:T(8,128)(2,1)} %param.11) | copy-start | bytes 6291460
  6.5 119.8 %all-gather.2.cloned.1.call-start = ((), (), s32[]{:S(2)}) async-start(), calls=%async_computation.3 | async-start | bytes 30277632 | tf_op jit(solution)/shard_map/all_gather | solution.py:60
  7.3 345.0 %reduce-scatter.2.cloned.1.call-start = ((), (), s32[]{:S(2)}) async-start(), calls=%async_computation.4 | async-start | bytes 5242880 | tf_op jit(solution)/shard_map/reduce_scatter | solution.py:70
  161.0 5.7 %copy-start.1 = (s32[4]{0:T(128)S(1)}, s32[4]{0:T(128)}, u32[]{:S(2)}) copy-start(s32[4]{0:T(128)} %param.9) | copy-start | bytes 52
  161.0 112.9 %all-to-all-start = ((bf16[4,2,128,3584]{3,2,1,0:T(8,128)(2,1)}), bf16[4,2,128,3584]{3,2,1,0:T(8,128)(2,1)}, u32[]{:S(2)}, u32[]{:S(2)}) async-start(bf16[4,2,128,3584]{3,2,1,0:T(8,128)(2,1)} %copy.19), calls=%async_computation.1 | async-start | bytes 14680064 | tf_op jit(solution)/shard_map/all_to_all | solution.py:78
Sparse Core Ops, SparseCore 0:
  9.5 116.7 all-gather.1
  149.5 70.9 reduce-scatter.1
where the time goes:
time: 366 us; the launch traced here: 362 us
  waiting for transfers between devices  223 us (61%)
  matrix products  43.7 us (12%)
  local copies, waits for them, and re-layouts  39.5 us (11%)
  blocking collectives  29.8 us (8%)
  between operations  14.1 us (4%)
  other arithmetic  6.08 us (2%)
  starting transfers between devices  5.77 us (2%)
    all_gather x1, waiting for transfers between devices, on_device(): lax.all_gather(down_weight, 'fsdp', axis=1, tiled=True)  117 us
    all_to_all x1, waiting for transfers between devices, on_device(): lax.all_to_all(outgoing, 'adapter', split_axis=0, concat_axis=3, tiled=True)  105 us
    all_to_all x1, blocking collectives, on_device(): lax.all_to_all(complete_delta, 'adapter', split_axis=3, concat_axis=0, ti...  29.8 us
    dot_general x1, matrix products, on_device(): jnp.dot(hidden, lax.all_gather(down_weight, 'fsdp', axis=1, tiled=True),...  23 us
    all_to_all x1, local copies, waits for them, and re-layouts, on_device(): lax.all_to_all(outgoing, 'adapter', split_axis=0, concat_axis=3, tiled=True)  11.8 us
    dot_general x1, matrix products, holder_delta(): lax.dot_general(rank_product, adapter_up_matrices[0], (((1,), (1,)), ((),...  10.3 us
    unnamed x5, local copies, waits for them, and re-layouts  7.91 us
  transfers between devices with their start and end apart: 3, of which 2 were waited for; matrix products, arithmetic and copies ran while one was open for 17% of the time, Pallas kernels for 0%

commit v1 on v0

v1 whole, which is shorter than its diff:
```python
import jax
import jax.numpy as jnp
from jax import lax
from jax.experimental import pallas as pl
from jax.experimental.pallas import tpu as pltpu
from jax.sharding import PartitionSpec as P

MESH = pl.DeviceIdType.MESH
ALPHA = 32.0
TILE = 128
TILES = 4
SLOTS = 2
N = 4
UNITS = 3584
HALF = UNITS // 2
QUART = UNITS // 4
COLS = 128
ROWS = TILES * TILE
RANK = 256
F32, BF16 = jnp.float32, jnp.bfloat16


def kernel(
    choice, ranks, h, w, a, b, out,
    held, own, sib, pack, land, a_v, b_v, part, d_send, d_recv, ring, fin_send, fin_recv, low, low_full,
    loc, w_send, w_recv, t_send, t_recv, s_send, s_recv, r_send, r_recv,
):
    f, z = lax.axis_index("fsdp"), lax.axis_index("adapter")
    x, y, c = f // 8, (f // 2) % N, f % 2

    def at(dx, dy):
        return (((x + dx + N) % N) * N + (y + dy + N) % N) * 2 + c, z

    def along(dz):
        return f, (z + dz + N) % N

    def blk(dx, dy):
        return ((x + dx + N) % N) * N + (y + dy + N) % N

    other = (x * N + y) * 2 + (1 - c), z
    me = blk(0, 0)

    own_copy = pltpu.make_async_copy(h, own, loc.at[0])
    own_copy.start()
    w_copy = pltpu.make_async_copy(w, held.at[me], loc.at[1])
    w_copy.start()
    a_copy = pltpu.make_async_copy(a, a_v, loc.at[2])
    a_copy.start()
    b_copy = pltpu.make_async_copy(b, b_v, loc.at[3])
    b_copy.start()

    barrier = pltpu.get_barrier_semaphore()
    friends = [at(1, 0), at(-1, 0), at(0, 1), at(0, -1), along(1), along(2), along(3), other]
    for friend in friends:
        pl.semaphore_signal(barrier, inc=1, device_id=friend, device_id_type=MESH)
    pl.semaphore_wait(barrier, len(friends))

    sent = []

    def remote(src, dst, s, r, device):
        copy = pltpu.make_async_remote_copy(
            src_ref=src, dst_ref=dst, send_sem=s, recv_sem=r, device_id=device, device_id_type=MESH
        )
        copy.start()
        sent.append(copy)
        return copy

    copies = {}

    def rows_of(way, piece):
        if piece is None:
            return pl.ds(way * HALF, HALF)
        return pl.ds(way * HALF + piece * QUART, QUART)

    def place(way, first, second):
        return (first, second) if way == 0 else (second, first)

    def push(key, way, origin, piece, step, source=None):
        spot = held.at[blk(*place(way, *origin)), rows_of(way, piece)]
        i = len(copies)
        copies[key] = remote(
            spot if source is None else source.at[rows_of(way, piece)],
            spot, w_send.at[i], w_recv.at[i], at(*place(way, *step)),
        )

    signs = (1, -1)
    for way in (0, 1):
        for sign in signs:
            push((1, way, sign), way, (0, 0), None, (sign, 0), w)
    for way in (0, 1):
        for sign in signs:
            push((3, way, 0, sign), way, (0, 0), None, (0, sign), w)

    sib_copy = remote(h, sib, s_send.at[0], s_recv.at[0], other)

    def slot_tile(holder, s):
        seen, found = jnp.int32(0), jnp.int32(0)
        for t in range(TILES):
            hit = (choice[t] == holder).astype(jnp.int32)
            found = found + jnp.where(seen == s, hit * t, 0)
            seen = seen + hit
        return found

    own_copy.wait()
    tiles = []
    for d in (2, 1, 3):
        holder = (z + d) % N
        for s in range(SLOTS):
            pack[d - 1, s] = own[slot_tile(holder, s)]
            tiles.append((d, s, remote(
                pack.at[d - 1, s], land.at[d - 1, s], t_send.at[d - 1, s], t_recv.at[d - 1, s], along(d)
            )))

    def multiply(first, second):
        both = jnp.concatenate([held[first], held[second]], axis=1)
        for rows, top in ((own, 0), (sib, ROWS)):
            r = jnp.dot(rows[...].reshape(ROWS, UNITS), both, preferred_element_type=F32).astype(BF16)
            part[first, pl.ds(top, ROWS)] = r[:, :COLS]
            part[second, pl.ds(top, ROWS)] = r[:, COLS:]

    def forward(way, o, sign):
        copies[(3, way, o, sign)].wait_recv()
        push((4, way, o, sign), way, (o, -sign), 0 if sign == 1 else 1, (0, sign))

    for way in (0, 1):
        for sign in signs:
            copies[(1, way, sign)].wait_recv()
            push((2, way, sign), way, (-sign, 0), 0 if sign == 1 else 1, (sign, 0))
    for way in (0, 1):
        for o in signs:
            for sign in signs:
                push((3, way, o, sign), way, (o, 0), None, (0, sign))
    for way in (0, 1):
        for sign in signs:
            forward(way, 0, sign)
    w_copy.wait()
    sib_copy.wait_recv()
    for way in (0, 1):
        for sign in signs:
            copies[(2, way, sign)].wait_recv()
        for sign in signs:
            push((3, way, 2, sign), way, (2, 0), None, (0, sign))
    multiply(blk(0, 0), blk(0, 1))
    for o in signs:
        for way in (0, 1):
            for sign in signs:
                forward(way, o, sign)

    @pl.loop(0, 2)
    def _(i):
        multiply(blk(2 * i - 1, 0), blk(2 * i - 1, 1))

    for way in (0, 1):
        for sign in signs:
            copies[(4, way, 0, sign)].wait_recv()
    multiply(blk(0, 3), blk(0, 2))

    for way in (0, 1):
        for sign in signs:
            forward(way, 2, sign)

    a_copy.wait()
    mine = [slot_tile(z, s) for s in range(SLOTS)]
    a_own = a_v[pl.ds(pl.multiple_of(z * UNITS, UNITS), UNITS)]
    for s in range(SLOTS):
        low[s] = jnp.dot(own[mine[s]], a_own, preferred_element_type=F32)

    for way in (0, 1):
        for o in (1, -1, 2):
            for sign in signs:
                copies[(4, way, o, sign)].wait_recv()

    @pl.loop(0, 4)
    def _(i):
        dx = jnp.where(i < 2, 2 * i - 1, 2)
        dy = jnp.where(i == 2, 0, 2)
        multiply(blk(dx, dy), blk(dx, dy + 1))

    for d in (1, 3, 2):
        for dd, s, copy in tiles:
            if dd == d:
                copy.wait_recv()
        source = (z - d + N) % N
        a_part = a_v[pl.ds(pl.multiple_of(source * UNITS, UNITS), UNITS)]
        r = jnp.dot(
            land[d - 1].reshape(SLOTS * TILE, UNITS), a_part, preferred_element_type=F32
        )
        for s in range(SLOTS):
            low[s] = low[s] + r[s * TILE:(s + 1) * TILE]

    rank = ranks[z]
    scale = ALPHA / rank.astype(F32)
    valid = lax.broadcasted_iota(jnp.int32, (TILE, RANK), 1) < rank
    for t in range(TILES):
        slot = jnp.int32(0)
        for before in range(t):
            slot = slot + (choice[before] == choice[t]).astype(jnp.int32)
        slot = jnp.minimum(slot, SLOTS - 1)
        keep = jnp.logical_and(valid, jnp.full((TILE, RANK), choice[t], jnp.int32) == z)
        low_full[pl.ds(t * TILE, TILE)] = jnp.where(keep, low[slot], 0.0).astype(BF16)

    b_copy.wait()

    def delta(q):
        @pl.loop(0, N)
        def _(k):
            at_rows = pl.ds(pl.multiple_of((q * N + k) * 2 * COLS, 2 * COLS), 2 * COLS)
            r = lax.dot_general(
                low_full[...], b_v[at_rows], (((1,), (1,)), ((), ())), preferred_element_type=F32
            ) * scale
            r = r.astype(BF16).astype(F32)
            even = jnp.full((ROWS, COLS), c, jnp.int32) == 0
            here = jnp.where(even, r[:, :COLS], r[:, COLS:])
            there = jnp.where(even, r[:, COLS:], r[:, :COLS])
            spot = part.at[q * N + k, pl.ds(0, ROWS)]
            spot[...] = (spot[...].astype(F32) + here).astype(BF16)
            d_send[q, k] = there.astype(BF16)

    def exchange(q, i):
        return remote(d_send.at[q], d_recv.at[q], s_send.at[1 + i], s_recv.at[1 + i], other)

    def take(q, copy):
        copy.wait_recv()

        @pl.loop(0, N)
        def _(k):
            spot = part.at[q * N + k, pl.ds(ROWS, ROWS)]
            spot[...] = (spot[...].astype(F32) + d_recv[q, k].astype(F32)).astype(BF16)

    hops = {}

    def hop(way, step, k):
        sign = 1 - 2 * way
        q = (z - sign * (1 + step) + 2 * N) % N
        spot = part.at[q * N + k, pl.ds(way * ROWS, ROWS)]
        if step:
            hops[(way, step - 1, k)].wait_recv()
            spot[...] = (spot[...].astype(F32) + ring[way, step - 1, k].astype(F32)).astype(BF16)
        hops[(way, step, k)] = remote(
            spot, ring.at[way, step, k], r_send.at[way, step, k], r_recv.at[way, step, k], along(sign)
        )

    below, above, far = (z + N - 1) % N, (z + 1) % N, (z + 2) % N
    delta(below)
    swap_below = exchange(below, 0)
    for k in range(N):
        hop(0, 0, k)
    delta(above)
    swap_above = exchange(above, 1)
    take(above, swap_above)
    for k in range(N):
        hop(1, 0, k)
    delta(far)
    swap_far = exchange(far, 2)
    delta(z)
    swap_own = exchange(z, 3)
    take(far, swap_far)
    for k in range(N):
        hop(0, 1, k)
        hop(1, 1, k)
    take(below, swap_below)
    take(z, swap_own)
    for k in range(N):
        hop(0, 2, k)
        hop(1, 2, k)
    last = []
    for k in range(N):
        for way in (1, 0):
            hops[(way, 2, k)].wait_recv()
            r = part[z * N + k, pl.ds(way * ROWS, ROWS)].astype(F32) + ring[way, 2, k].astype(F32)
            if way:
                fin_send[k] = r.astype(BF16)
                last.append(remote(fin_send.at[k], fin_recv.at[k], s_send.at[5 + k], s_recv.at[5 + k], other))
            else:
                out[:, pl.ds(pl.multiple_of((2 * k + c) * COLS, COLS), COLS)] = r.astype(BF16)
    for k in range(N):
        last[k].wait_recv()
        out[:, pl.ds(pl.multiple_of((2 * k + 1 - c) * COLS, COLS), COLS)] = fin_recv[k]
    for copy in sent:
        copy.wait_send()


def on_device(hidden, down_weight, choice, ranks, down, up):
    anywhere = pl.BlockSpec(memory_space=pl.ANY)
    small = pl.BlockSpec(memory_space=pltpu.SMEM)
    tiles = hidden.reshape(TILES, TILE, UNITS)
    dma = pltpu.SemaphoreType.DMA
    return pl.pallas_call(
        kernel,
        out_shape=jax.ShapeDtypeStruct((ROWS, N * 2 * COLS), BF16),
        in_specs=[small, small, anywhere, anywhere, anywhere, anywhere],
        out_specs=pl.BlockSpec(memory_space=pltpu.VMEM),
        scratch_shapes=[
            pltpu.VMEM((N * N, UNITS, COLS), BF16),
            pltpu.VMEM((TILES, TILE, UNITS), BF16),
            pltpu.VMEM((TILES, TILE, UNITS), BF16),
            pltpu.VMEM((N - 1, SLOTS, TILE, UNITS), BF16),
            pltpu.VMEM((N - 1, SLOTS, TILE, UNITS), BF16),
            pltpu.VMEM((N * UNITS, RANK), BF16),
            pltpu.VMEM((N * N * 2 * COLS, RANK), BF16),
            pltpu.VMEM((N * N, 2 * ROWS, COLS), BF16),
            pltpu.VMEM((N, N, ROWS, COLS), BF16),
            pltpu.VMEM((N, N, ROWS, COLS), BF16),
            pltpu.VMEM((2, 3, N, ROWS, COLS), BF16),
            pltpu.VMEM((N, ROWS, COLS), BF16),
            pltpu.VMEM((N, ROWS, COLS), BF16),
            pltpu.VMEM((SLOTS, TILE, RANK), F32),
            pltpu.VMEM((ROWS, RANK), BF16),
            dma((4,)),
            dma((40,)),
            dma((40,)),
            dma((N - 1, SLOTS)),
            dma((N - 1, SLOTS)),
            dma((9,)),
            dma((9,)),
            dma((2, 3, N)),
            dma((2, 3, N)),
        ],
        compiler_params=pltpu.CompilerParams(
            collective_id=0, has_side_effects=True, vmem_limit_bytes=62 * 2**20
        ),
        cost_estimate=pl.CostEstimate(
            flops=20_000_000_000, bytes_accessed=15_000_000, transcendentals=0
        ),
    )(choice.reshape(TILES), ranks, tiles, down_weight, down[0], up[0])


def solution(mesh):
    return jax.shard_map(
        on_device,
        mesh=mesh,
        in_specs=(
            P("fsdp", "adapter"),
            P("adapter", "fsdp"),
            P("fsdp", None),
            P("fsdp"),
            P(("fsdp", "adapter"), None, None),
            P(("fsdp", "adapter"), None, None),
        ),
        out_specs=P("fsdp", "adapter"),
        check_vma=False,
    )
```

time: 366 us -> 139 us (0.38)
  waiting for transfers between devices: 223 us -> 0 us
  Pallas kernels: 0 us -> 134 us
  matrix products: 43.7 us -> 0 us
  local copies, waits for them, and re-layouts: 39.5 us -> 2.26 us
  blocking collectives: 29.8 us -> 0 us
  between operations: 14.1 us -> 0.01 us
  other arithmetic: 6.08 us -> 0 us
  starting transfers between devices: 5.77 us -> 0 us
    pallas_call x0 -> x1, Pallas kernels: none -> 134 us  [on_device(): pl.pallas_call(kernel, out_shape=jax.ShapeDtypeStruct((ROWS, N * 2 * COLS...]
    all_gather x1 -> x0, waiting for transfers between devices: 117 us -> none  [on_device(): lax.all_gather(down_weight, 'fsdp', axis=1, tiled=True)]
    all_to_all x1 -> x0, waiting for transfers between devices: 105 us -> none  [on_device(): lax.all_to_all(outgoing, 'adapter', split_axis=0, concat_axis=3, tiled=True)]
    dot_general x4 -> x0, matrix products: 43.7 us -> none  [the longest x1 23 us: on_device(): jnp.dot(hidden, lax.all_gather(down_weight, 'fsdp', axis=1, tiled=True),...]
    all_to_all x1 -> x0, blocking collectives: 29.8 us -> none  [on_device(): lax.all_to_all(complete_delta, 'adapter', split_axis=3, concat_axis=0, ti...]
    all_to_all x2 -> x0, local copies, waits for them, and re-layouts: 18.3 us -> none  [the longest x1 11.8 us: on_device(): lax.all_to_all(outgoing, 'adapter', split_axis=0, concat_axis=3, tiled=True)]
    reshape x1 -> x0, local copies, waits for them, and re-layouts: 6.15 us -> none  [holder_delta(): complete_delta.astype(jnp.bfloat16)]
    all_to_all x1 -> x0, starting transfers between devices: 5.72 us -> none  [on_device(): lax.all_to_all(outgoing, 'adapter', split_axis=0, concat_axis=3, tiled=True)]
  transfers between devices with their start and end apart: 3 -> 0, of which waited for: 2 -> 0; matrix products, arithmetic and copies ran while one was open for 17% -> 0% of each run, Pallas kernels for 0% -> 0%
where the time goes in v1:
time: 139 us; the launch traced here: 137 us
  Pallas kernels  134 us (96%)
  local copies, waits for them, and re-layouts  2.26 us (2%)
    pallas_call x1, Pallas kernels, on_device(): pl.pallas_call(kernel, out_shape=jax.ShapeDtypeStruct((ROWS, N * 2 * COLS...  134 us

profile of v1, /device:TPU:39, one launch (start us, length us, event | category | flops | bytes accessed | tf_op | source)
XLA Modules:
  0.0 136.5 jit_solution(10951497042430917514)
XLA Ops:
  0.0 134.3 %shard_map.64 = bf16[512,1024]{1,0:T(8,128)(2,1)} custom-call(s32[4]{0:T(128)} %bitcast.7, s32[4]{0:T(128)} %ranks.1, bf16[4,128,3584]{2,1,0:T(8,128)(2,1)} %bitcast.5, bf16[3584,128]{1,0:T(8,128)(2,1)} %w.1, bf16[14336,256]{1,0:T(8,128)(2,1)} %bitcast.4, bf16[4096,256]{1,0:T(8,128)(2,1)} %bitcast.6), custom_call_target="tpu_custom_call" | custom-call | flops 20000000000 | bytes 15000000 | tf_op jit(solution)/shard_map/pallas_call | solution.py:288
  134.3 2.3 %copy.8 = bf16[512,1024]{1,0:T(8,128)(2,1)} copy(bf16[512,1024]{1,0:T(8,128)(2,1)} %shard_map.64) | data formatting | bytes 2097152

commit v2 on v1

v2 whole, which is shorter than its diff:
```python
import functools

import jax
import jax.numpy as jnp
import numpy as np
from jax import lax
from jax.experimental import pallas as pl
from jax.experimental.pallas import tpu as pltpu
from jax.sharding import PartitionSpec as P

MESH = pl.DeviceIdType.MESH
ALPHA = 32.0
TILE = 128
TILES = 4
SLOTS = 2
N = 4
UNITS = 3584
HALF = UNITS // 2
QUART = UNITS // 4
COLS = 128
ROWS = TILES * TILE
RANK = 256
PARTS = QUART // COLS
STEPS = 10
LAG = 2
WIDTH = 4 * STEPS + 2
F32, BF16 = jnp.float32, jnp.bfloat16

CLASSES = (
    ((1, 1, 1, 1), {0: 3, 1: 2, 2: 1, 3: 0}, ()),
    ((2, 2, 0, 0), {}, ((0, 2, 3, 3), (1, 3, 2, 2))),
    ((2, 0, 2, 0), {0: 1, 2: 3}, ((0, 1, 1, 1), (2, 3, 3, 3))),
    ((2, 1, 1, 0), {0: 3, 1: 2, 2: 1}, ((0, 3, 3, 3),)),
    ((2, 0, 1, 1), {0: 1, 2: 3, 3: 2}, ((0, 1, 1, 1),)),
    ((2, 1, 0, 1), {1: 2, 3: 2}, ((0, 2, 1, 3),)),
)
TILE_KIND, MATRIX_KIND, PASS_ON = 64, 128, 256


@functools.cache
def routes():
    table = np.zeros(81 + len(CLASSES) * N * WIDTH, np.int32)
    for index, (counts, via, moved) in enumerate(CLASSES):
        for turn in reversed(range(N)):
            code = 0
            for i in range(N):
                code = code * 3 + counts[(i - turn) % N]
            table[code] = index * N + turn
        rows = table[81 + index * N * WIDTH:81 + (index + 1) * N * WIDTH].reshape(N, WIDTH)
        send = np.zeros((N, 2, STEPS), np.int32)
        take = np.zeros((N, 2, STEPS), np.int32)
        flows = []
        away = {(o, s) for o, s, _, _ in moved}
        for o, s, first, second in moved:
            rows[s, 4 * STEPS] = (o - s) % N
            rows[o, 4 * STEPS + 1] |= 1 << ((s - o) % N)
            for half, by in enumerate((first, second)):
                path = (o, s) if by == s else (o, by, s)
                flows.append((path, MATRIX_KIND + (s - o) % N * 8 + half * 4, MATRIX_KIND + (o - s) % N * 8 + half * 4))
        for o in range(N):
            for s in range(N):
                if s == o or (o, s) in away:
                    continue
                for slot in range(counts[o]):
                    path = (s, via[o], o) if (s - o) % N == 2 else (s, o)
                    flows.append((path, TILE_KIND + (o - s) % N * 8 + slot * 4, TILE_KIND + (s - o) % N * 8 + slot * 4))
        flows.sort(key=lambda flow: -len(flow[0]))
        for path, code_send, code_take in flows:
            link = 0 if (path[1] - path[0]) % N == 1 else 1
            for k in range(4):
                p = 0
                while send[path[0], link, p] or (len(path) == 3 and send[path[1], link, p + LAG]):
                    p += 1
                send[path[0], link, p] = code_send + k
                if len(path) == 3:
                    p += LAG
                    send[path[1], link, p] = PASS_ON
                take[path[-1], link, p] = code_take + k
        rows[:, :2 * STEPS] = send.reshape(N, -1)
        rows[:, 2 * STEPS:4 * STEPS] = take.reshape(N, -1)
    return table


def kernel(
    choice, ranks, table, h, w, a, b, out,
    held, own, sib, pool, outgo, income, b_v, part, d_own, d_send, d_recv, ring, fin_send, fin_recv,
    low, away, away_send, away_recv, low_full,
    loc, w_send, w_recv, t_send, t_recv, s_send, s_recv, f_send, f_recv, r_send, r_recv,
):
    f, z = lax.axis_index("fsdp"), lax.axis_index("adapter")
    x, y, c = f // 8, (f // 2) % N, f % 2

    def at(dx, dy):
        return (((x + dx + N) % N) * N + (y + dy + N) % N) * 2 + c, z

    def along(dz):
        return f, (z + dz + N) % N

    def blk(dx, dy):
        return ((x + dx + N) % N) * N + (y + dy + N) % N

    other = (x * N + y) * 2 + (1 - c), z
    me = blk(0, 0)

    own_copy = pltpu.make_async_copy(h, own, loc.at[0])
    own_copy.start()
    a_copies = []
    for half in range(2):
        a_copies.append(pltpu.make_async_copy(
            a.at[:, :, pl.ds(half * COLS, COLS)], pool.at[pl.ds(16 + 16 * half, 16)], loc.at[1 + half]
        ))
        a_copies[half].start()
    w_copy = pltpu.make_async_copy(w, held.at[me], loc.at[3])
    w_copy.start()

    barrier = pltpu.get_barrier_semaphore()
    friends = [at(1, 0), at(-1, 0), at(0, 1), at(0, -1), along(1), along(2), along(3), other]
    for friend in friends:
        pl.semaphore_signal(barrier, inc=1, device_id=friend, device_id_type=MESH)
    pl.semaphore_wait(barrier, len(friends))

    sent = []

    def describe(src, dst, s, r, device):
        return pltpu.make_async_remote_copy(
            src_ref=src, dst_ref=dst, send_sem=s, recv_sem=r, device_id=device, device_id_type=MESH
        )

    def remote(src, dst, s, r, device):
        copy = describe(src, dst, s, r, device)
        copy.start()
        sent.append(copy)
        return copy

    copies = {}

    def rows_of(way, piece):
        if piece is None:
            return pl.ds(way * HALF, HALF)
        return pl.ds(way * HALF + piece * QUART, QUART)

    def place(way, first, second):
        return (first, second) if way == 0 else (second, first)

    def push(key, way, origin, piece, step, source=None):
        spot = held.at[blk(*place(way, *origin)), rows_of(way, piece)]
        i = len(copies)
        copies[key] = remote(
            spot if source is None else source.at[rows_of(way, piece)],
            spot, w_send.at[i], w_recv.at[i], at(*place(way, *step)),
        )

    def forward(way, o, sign):
        copies[(3, way, o, sign)].wait_recv()
        push((4, way, o, sign), way, (o, -sign), 0 if sign == 1 else 1, (0, sign))

    signs = (1, -1)
    for way in (0, 1):
        for sign in signs:
            push((1, way, sign), way, (0, 0), None, (sign, 0), w)
    for way in (0, 1):
        for sign in signs:
            push((3, way, 0, sign), way, (0, 0), None, (0, sign), w)

    sib_copy = remote(h, sib, s_send.at[0], s_recv.at[0], other)

    def slot_tile(holder, s):
        seen, found = jnp.int32(0), jnp.int32(0)
        for t in range(TILES):
            hit = (choice[t] == holder).astype(jnp.int32)
            found = found + jnp.where(seen == s, hit * t, 0)
            seen = seen + hit
        return found

    code = jnp.int32(0)
    for o in range(N):
        count = jnp.int32(0)
        for t in range(TILES):
            count = count + (choice[t] == o).astype(jnp.int32)
        code = code * 3 + count
    found = table[code]
    base = 81 + ((found // N) * N + (z - found % N + N) % N) * WIDTH

    def fields(entry):
        return (z + entry % 64 // 8) % N, entry // 4 % 2, entry % 4

    def matrix(piece, half, k):
        return 16 + half * 16 + piece * 4 + k

    def z_copy(link, j):
        return describe(
            outgo.at[link, j], income.at[link, j], t_send.at[link, j], t_recv.at[link, j], along(1 - 2 * link)
        )

    def step(j, first):
        for link in range(2):
            entry = table[base + link * STEPS + j]
            piece, which, k = fields(entry)
            is_matrix = jnp.logical_and(entry >= MATRIX_KIND, entry < PASS_ON)
            value = pool[jnp.where(is_matrix, matrix(piece, which, k), slot_tile(piece, which) * 4 + k)]
            if not first:
                value = lax.select(entry == PASS_ON, income[link, j - LAG], value)
            outgo[link, j] = value
            z_copy(link, j).start()

    def wide(piece):
        return jnp.concatenate([piece[i * COLS:(i + 1) * COLS] for i in range(PARTS)], axis=1)

    def matrix_rows(piece, k):
        return jnp.concatenate([pool[matrix(piece, half, k)] for half in range(2)], axis=1)

    def use(j):
        for link in range(2):
            entry = table[base + (2 + link) * STEPS + j]
            piece, which, k = fields(entry)
            got = income[link, j]
            r = jnp.dot(wide(got), matrix_rows(piece, k), preferred_element_type=F32)
            for s in range(SLOTS):
                ok = jnp.logical_and(entry // 64 == 1, which == s)
                low[s] = low[s] + lax.select(ok, r, jnp.zeros_like(r))
            rows = jnp.concatenate([wide(pool[slot_tile(piece, s) * 4 + k]) for s in range(SLOTS)], axis=0)
            r = jnp.dot(rows, got, preferred_element_type=F32)
            for half in range(2):
                ok = jnp.logical_and(entry // 64 == 2, which == half)
                away[half] = away[half] + lax.select(ok, r, jnp.zeros_like(r))

    def exchange(lo, hi):
        @pl.loop(lo, hi)
        def _(j):
            for link in range(2):
                z_copy(link, j - LAG).wait_recv()
            step(j, False)
            use(j - LAG)

    def multiply(first, second):
        both = jnp.concatenate([held[first], held[second]], axis=1)
        for rows, top in ((own, 0), (sib, ROWS)):
            r = jnp.dot(rows[...].reshape(ROWS, UNITS), both, preferred_element_type=F32).astype(BF16)
            part[first, pl.ds(top, ROWS)] = r[:, :COLS]
            part[second, pl.ds(top, ROWS)] = r[:, COLS:]

    own_copy.wait()

    @pl.loop(0, TILES)
    def _(t):
        for i in range(UNITS // COLS):
            pool[t * 4 + i // PARTS, pl.ds(i % PARTS * COLS, COLS)] = own[t, :, i * COLS:(i + 1) * COLS]

    for copy in a_copies:
        copy.wait()
    for j in range(LAG):
        step(j, True)
    b_copy = pltpu.make_async_copy(b, b_v, loc.at[4])
    b_copy.start()
    away[...] = jnp.zeros_like(away)
    low[...] = jnp.zeros_like(low)
    mine = [slot_tile(z, s) for s in range(SLOTS)]

    @pl.loop(0, 4)
    def _(k):
        rows = jnp.concatenate([wide(pool[mine[s] * 4 + k]) for s in range(SLOTS)], axis=0)
        r = jnp.dot(rows, matrix_rows(z, k), preferred_element_type=F32)
        for s in range(SLOTS):
            low[s] = low[s] + r[s * TILE:(s + 1) * TILE]

    exchange(2, 5)
    for way in (0, 1):
        for sign in signs:
            copies[(1, way, sign)].wait_recv()
            push((2, way, sign), way, (-sign, 0), 0 if sign == 1 else 1, (sign, 0))
    for way in (0, 1):
        for o in signs:
            for sign in signs:
                push((3, way, o, sign), way, (o, 0), None, (0, sign))
    for way in (0, 1):
        for sign in signs:
            forward(way, 0, sign)
    exchange(5, 7)
    w_copy.wait()
    sib_copy.wait_recv()
    multiply(blk(0, 0), blk(1, 0))
    exchange(7, 9)
    multiply(blk(0, 1), blk(0, -1))
    exchange(9, 10)
    for way in (0, 1):
        for sign in signs:
            copies[(2, way, sign)].wait_recv()
        for sign in signs:
            push((3, way, 2, sign), way, (2, 0), None, (0, sign))
    for j in range(STEPS - LAG, STEPS):
        for link in range(2):
            z_copy(link, j).wait_recv()
        use(j)

    for half in range(2):
        away_send[half] = away[half].astype(BF16)
    returns = [
        remote(away_send, away_recv.at[d - 1], f_send.at[d - 1], f_recv.at[d - 1], along(d)) for d in (2, 1, 3)
    ]
    for o in signs:
        for way in (0, 1):
            for sign in signs:
                forward(way, o, sign)
    multiply(blk(-1, 0), blk(1, 1))
    for copy in returns:
        copy.wait_recv()
    flags = table[base + 4 * STEPS + 1]
    for d in (1, 2, 3):
        ok = flags // (1 << (N - d)) % 2 == 1
        for s in range(SLOTS):
            for half in range(2):
                r = away_recv[d - 1, half, s * TILE:(s + 1) * TILE].astype(F32)
                spot = low.at[s, :, half * COLS:(half + 1) * COLS]
                spot[...] = spot[...] + lax.select(ok, r, jnp.zeros_like(r))

    rank = ranks[z]
    scale = ALPHA / rank.astype(F32)
    valid = lax.broadcasted_iota(jnp.int32, (TILE, RANK), 1) < rank
    for t in range(TILES):
        slot = jnp.int32(0)
        for before in range(t):
            slot = slot + (choice[before] == choice[t]).astype(jnp.int32)
        slot = jnp.minimum(slot, SLOTS - 1)
        keep = jnp.logical_and(valid, jnp.full((TILE, RANK), choice[t], jnp.int32) == z)
        low_full[pl.ds(t * TILE, TILE)] = jnp.where(keep, low[slot], 0.0).astype(BF16)

    b_copy.wait()
    swaps = []
    for q in range(N):
        @pl.loop(0, N)
        def _(k):
            at_rows = pl.ds(pl.multiple_of((q * N + k) * 2 * COLS, 2 * COLS), 2 * COLS)
            r = lax.dot_general(
                low_full[...], b_v[at_rows], (((1,), (1,)), ((), ())), preferred_element_type=F32
            ) * scale
            r = r.astype(BF16)
            d_own[q * N + k] = lax.select(c == 0, r[:, :COLS], r[:, COLS:])
            d_send[q * N + k] = lax.select(c == 0, r[:, COLS:], r[:, :COLS])

        here = pl.ds(q * N, N)
        swaps.append(remote(d_send.at[here], d_recv.at[here], s_send.at[1 + q], s_recv.at[1 + q], other))

    def role(way, dx):
        q = (x + dx + N) % N
        return ((z - q - 1) if way == 0 else (q - 1 - z)) % N

    def hop(way, block):
        b_at = blk(*block)
        return describe(
            part.at[b_at, pl.ds(way * ROWS, ROWS)], ring.at[way, b_at],
            r_send.at[way, b_at], r_recv.at[way, b_at], along(1 - 2 * way),
        )

    def finish(block):
        k = (y + block[1] + N) % N
        return describe(fin_send.at[k], fin_recv.at[k], s_send.at[5 + k], s_recv.at[5 + k], other)

    def act(way, block, turn):
        @pl.when(role(way, block[0]) == turn)
        def _():
            b_at = blk(*block)
            k = (y + block[1] + N) % N
            if turn:
                hop(way, block).wait_recv()

            @pl.loop(0, TILES)
            def _(i):
                some = pl.ds(pl.multiple_of(i * TILE, TILE), TILE)
                spot = part.at[b_at, pl.ds(pl.multiple_of(way * ROWS + i * TILE, TILE), TILE)]
                r = spot[...].astype(F32) + (d_recv if way else d_own)[b_at, some].astype(F32)
                if turn:
                    r = r + ring[way, b_at, some].astype(F32)
                r = r.astype(BF16)
                if turn < 3:
                    spot[...] = r
                elif way:
                    fin_send[k, some] = r
                else:
                    out[some, pl.ds(pl.multiple_of((2 * k + c) * COLS, COLS), COLS)] = r

            if turn < 3:
                hop(way, block).start()
            elif way:
                finish(block).start()

    order = (
        (0, 0), (1, 0), (0, 1), (0, -1), (-1, 0), (1, 1), (1, -1), (-1, 1), (-1, -1), (2, 0),
        (0, 2), (1, 2), (-1, 2), (2, 1), (2, -1), (2, 2),
    )

    def point(p):
        for turn in (3, 2, 1, 0):
            i = p - 2 * turn
            if 0 <= i < 8:
                for block in order[2 * i:2 * i + 2]:
                    for way in (1, 0):
                        act(way, block, turn)

    multiply(blk(1, -1), blk(-1, 1))
    for way in (0, 1):
        for sign in signs:
            copies[(4, way, 0, sign)].wait_recv()
    multiply(blk(-1, -1), blk(2, 0))
    for copy in swaps:
        copy.wait_recv()
    point(0)
    point(1)
    for way in (0, 1):
        for sign in signs:
            forward(way, 2, sign)
    point(2)
    point(3)
    point(4)
    for way in (0, 1):
        for o in signs:
            for sign in signs:
                copies[(4, way, o, sign)].wait_recv()
    multiply(blk(0, 2), blk(1, 2))
    point(5)
    multiply(blk(-1, 2), blk(2, 1))
    point(6)
    for way in (0, 1):
        for sign in signs:
            copies[(4, way, 2, sign)].wait_recv()
    multiply(blk(2, -1), blk(2, 2))
    for p in range(7, 14):
        point(p)
    for block in order:
        @pl.when(role(1, block[0]) == 3)
        def _():
            k = (y + block[1] + N) % N
            finish(block).wait()
            out[:, pl.ds(pl.multiple_of((2 * k + 1 - c) * COLS, COLS), COLS)] = fin_recv[k]

        for way in (0, 1):
            @pl.when(role(way, block[0]) != 3)
            def _():
                hop(way, block).wait_send()

    @pl.loop(0, STEPS)
    def _(j):
        for link in range(2):
            z_copy(link, j).wait_send()

    for copy in sent:
        copy.wait_send()


def on_device(hidden, down_weight, choice, ranks, down, up):
    anywhere = pl.BlockSpec(memory_space=pl.ANY)
    small = pl.BlockSpec(memory_space=pltpu.SMEM)
    tiles = hidden.reshape(TILES, TILE, UNITS)
    matrix = down.reshape(4 * N, QUART, RANK)
    dma = pltpu.SemaphoreType.DMA
    return pl.pallas_call(
        kernel,
        out_shape=jax.ShapeDtypeStruct((ROWS, N * 2 * COLS), BF16),
        in_specs=[small, small, small, anywhere, anywhere, anywhere, anywhere],
        out_specs=pl.BlockSpec(memory_space=pltpu.VMEM),
        scratch_shapes=[
            pltpu.VMEM((N * N, UNITS, COLS), BF16),
            pltpu.VMEM((TILES, TILE, UNITS), BF16),
            pltpu.VMEM((TILES, TILE, UNITS), BF16),
            pltpu.VMEM((48, QUART, COLS), BF16),
            pltpu.VMEM((2, STEPS, QUART, COLS), BF16),
            pltpu.VMEM((2, STEPS, QUART, COLS), BF16),
            pltpu.VMEM((N * N * 2 * COLS, RANK), BF16),
            pltpu.VMEM((N * N, 2 * ROWS, COLS), BF16),
            pltpu.VMEM((N * N, ROWS, COLS), BF16),
            pltpu.VMEM((N * N, ROWS, COLS), BF16),
            pltpu.VMEM((N * N, ROWS, COLS), BF16),
            pltpu.VMEM((2, N * N, ROWS, COLS), BF16),
            pltpu.VMEM((N, ROWS, COLS), BF16),
            pltpu.VMEM((N, ROWS, COLS), BF16),
            pltpu.VMEM((SLOTS, TILE, RANK), F32),
            pltpu.VMEM((2, SLOTS * TILE, COLS), F32),
            pltpu.VMEM((2, SLOTS * TILE, COLS), BF16),
            pltpu.VMEM((N - 1, 2, SLOTS * TILE, COLS), BF16),
            pltpu.VMEM((ROWS, RANK), BF16),
            dma((5,)),
            dma((40,)),
            dma((40,)),
            dma((2, STEPS)),
            dma((2, STEPS)),
            dma((9,)),
            dma((9,)),
            dma((N - 1,)),
            dma((N - 1,)),
            dma((2, N * N)),
            dma((2, N * N)),
        ],
        compiler_params=pltpu.CompilerParams(
            collective_id=0, has_side_effects=True, vmem_limit_bytes=63 * 2**20
        ),
        cost_estimate=pl.CostEstimate(
            flops=20_000_000_000, bytes_accessed=15_000_000, transcendentals=0
        ),
    )(choice.reshape(TILES), ranks, jnp.asarray(routes()), tiles, down_weight, matrix, up[0])


def solution(mesh):
    return jax.shard_map(
        on_device,
        mesh=mesh,
        in_specs=(
            P("fsdp", "adapter"),
            P("adapter", "fsdp"),
            P("fsdp", None),
            P("fsdp"),
            P(("fsdp", "adapter"), None, None),
            P(("fsdp", "adapter"), None, None),
        ),
        out_specs=P("fsdp", "adapter"),
        check_vma=False,
    )
```

time: 139 us -> 130 us (0.935)
  Pallas kernels: 134 us -> 125 us
    pallas_call x1, Pallas kernels: 134 us -> 125 us  [on_device(): pl.pallas_call(kernel, out_shape=jax.ShapeDtypeStruct((ROWS, N * 2 * COLS...]
where the time goes in v2:
time: 130 us; the launch traced here: 128 us
  Pallas kernels  125 us (96%)
  local copies, waits for them, and re-layouts  2.26 us (2%)
    pallas_call x1, Pallas kernels, on_device(): pl.pallas_call(kernel, out_shape=jax.ShapeDtypeStruct((ROWS, N * 2 * COLS...  125 us

profile of v2, /device:TPU:39, one launch (start us, length us, event | category | flops | bytes accessed | tf_op | source)
XLA Modules:
  0.0 127.8 jit_solution(11933347719808828303)
XLA Ops:
  0.0 125.5 %shard_map.73 = bf16[512,1024]{1,0:T(8,128)(2,1)} custom-call(s32[4]{0:T(128)} %bitcast.7, s32[4]{0:T(128)} %ranks.1, s32[1089]{0:T(1024)} %constant.2.clone.table, bf16[4,128,3584]{2,1,0:T(8,128)(2,1)} %bitcast.5, bf16[3584,128]{1,0:T(8,128)(2,1)} %w.1, bf16[16,896,256]{2,1,0:T(8,128)(2,1)} %bitcast.4, bf16[4096,256]{1,0:T(8,128)(2,1)} %bitcast.6), custom_call_target="tpu_custom_call" | custom-call | flops 20000000000 | bytes 15000000 | tf_op jit(solution)/shard_map/pallas_call | solution.py:455
  125.5 2.3 %copy.9 = bf16[512,1024]{1,0:T(8,128)(2,1)} copy(bf16[512,1024]{1,0:T(8,128)(2,1)} %shard_map.73) | data formatting | bytes 2097152

commit v3 on v2

--- a/solution.py
+++ b/solution.py
@@ -20,15 +20,17 @@
 COLS = 128
 ROWS = TILES * TILE
 RANK = 256
-PARTS = QUART // COLS
-STEPS = 10
-LAG = 2
+CHUNK = 512
+CHUNKS = UNITS // CHUNK
+PARTS = CHUNK // COLS
+LAG = 3
+STEPS = SLOTS * CHUNKS + LAG
 WIDTH = 4 * STEPS + 2
 F32, BF16 = jnp.float32, jnp.bfloat16
 
 CLASSES = (
     ((1, 1, 1, 1), {0: 3, 1: 2, 2: 1, 3: 0}, ()),
-    ((2, 2, 0, 0), {}, ((0, 2, 3, 3), (1, 3, 2, 2))),
+    ((2, 2, 0, 0), {0: 3, 1: 2}, ((0, 3, 3, 3), (1, 2, 2, 2))),
     ((2, 0, 2, 0), {0: 1, 2: 3}, ((0, 1, 1, 1), (2, 3, 3, 3))),
     ((2, 1, 1, 0), {0: 3, 1: 2, 2: 1}, ((0, 3, 3, 3),)),
     ((2, 0, 1, 1), {0: 1, 2: 3, 3: 2}, ((0, 1, 1, 1),)),
@@ -56,18 +58,18 @@
             rows[o, 4 * STEPS + 1] |= 1 << ((s - o) % N)
             for half, by in enumerate((first, second)):
                 path = (o, s) if by == s else (o, by, s)
-                flows.append((path, MATRIX_KIND + (s - o) % N * 8 + half * 4, MATRIX_KIND + (o - s) % N * 8 + half * 4))
+                flows.append((path, MATRIX_KIND + (s - o) % N * 16 + half * 8, MATRIX_KIND + (o - s) % N * 16 + half * 8))
         for o in range(N):
             for s in range(N):
                 if s == o or (o, s) in away:
                     continue
                 for slot in range(counts[o]):
                     path = (s, via[o], o) if (s - o) % N == 2 else (s, o)
-                    flows.append((path, TILE_KIND + (o - s) % N * 8 + slot * 4, TILE_KIND + (s - o) % N * 8 + slot * 4))
+                    flows.append((path, TILE_KIND + (o - s) % N * 16 + slot * 8, TILE_KIND + (s - o) % N * 16 + slot * 8))
         flows.sort(key=lambda flow: -len(flow[0]))
         for path, code_send, code_take in flows:
             link = 0 if (path[1] - path[0]) % N == 1 else 1
-            for k in range(4):
+            for k in range(CHUNKS):
                 p = 0
                 while send[path[0], link, p] or (len(path) == 3 and send[path[1], link, p + LAG]):
                     p += 1
@@ -107,7 +109,7 @@
     a_copies = []
     for half in range(2):
         a_copies.append(pltpu.make_async_copy(
-            a.at[:, :, pl.ds(half * COLS, COLS)], pool.at[pl.ds(16 + 16 * half, 16)], loc.at[1 + half]
+            a.at[:, :, pl.ds(half * COLS, COLS)], pool.at[pl.ds((1 + half) * N * CHUNKS, N * CHUNKS)], loc.at[1 + half]
         ))
         a_copies[half].start()
     w_copy = pltpu.make_async_copy(w, held.at[me], loc.at[3])
@@ -117,6 +119,13 @@
     friends = [at(1, 0), at(-1, 0), at(0, 1), at(0, -1), along(1), along(2), along(3), other]
     for friend in friends:
         pl.semaphore_signal(barrier, inc=1, device_id=friend, device_id_type=MESH)
+    own_copy.wait()
+
+    @pl.loop(0, TILES)
+    def _(t):
+        for i in range(UNITS // COLS):
+            pool[t * CHUNKS + i // PARTS, pl.ds(i % PARTS * COLS, COLS)] = own[t, :, i * COLS:(i + 1) * COLS]
+
     pl.semaphore_wait(barrier, len(friends))
 
     sent = []
@@ -182,10 +191,10 @@
     base = 81 + ((found // N) * N + (z - found % N + N) % N) * WIDTH
 
     def fields(entry):
-        return (z + entry % 64 // 8) % N, entry // 4 % 2, entry % 4
+        return (z + entry % 64 // 16) % N, entry // 8 % 2, jnp.minimum(entry % 8, CHUNKS - 1)
 
     def matrix(piece, half, k):
-        return 16 + half * 16 + piece * 4 + k
+        return TILES * CHUNKS + (half * N + piece) * CHUNKS + k
 
     def z_copy(link, j):
         return describe(
@@ -197,7 +206,7 @@
             entry = table[base + link * STEPS + j]
             piece, which, k = fields(entry)
             is_matrix = jnp.logical_and(entry >= MATRIX_KIND, entry < PASS_ON)
-            value = pool[jnp.where(is_matrix, matrix(piece, which, k), slot_tile(piece, which) * 4 + k)]
+            value = pool[jnp.where(is_matrix, matrix(piece, which, k), slot_tile(piece, which) * CHUNKS + k)]
             if not first:
                 value = lax.select(entry == PASS_ON, income[link, j - LAG], value)
             outgo[link, j] = value
@@ -218,7 +227,7 @@
             for s in range(SLOTS):
                 ok = jnp.logical_and(entry // 64 == 1, which == s)
                 low[s] = low[s] + lax.select(ok, r, jnp.zeros_like(r))
-            rows = jnp.concatenate([wide(pool[slot_tile(piece, s) * 4 + k]) for s in range(SLOTS)], axis=0)
+            rows = jnp.concatenate([wide(pool[slot_tile(piece, s) * CHUNKS + k]) for s in range(SLOTS)], axis=0)
             r = jnp.dot(rows, got, preferred_element_type=F32)
             for half in range(2):
                 ok = jnp.logical_and(entry // 64 == 2, which == half)
@@ -238,13 +247,6 @@
             r = jnp.dot(rows[...].reshape(ROWS, UNITS), both, preferred_element_type=F32).astype(BF16)
             part[first, pl.ds(top, ROWS)] = r[:, :COLS]
             part[second, pl.ds(top, ROWS)] = r[:, COLS:]
-
-    own_copy.wait()
-
-    @pl.loop(0, TILES)
-    def _(t):
-        for i in range(UNITS // COLS):
-            pool[t * 4 + i // PARTS, pl.ds(i % PARTS * COLS, COLS)] = own[t, :, i * COLS:(i + 1) * COLS]
 
     for copy in a_copies:
         copy.wait()
@@ -256,14 +258,14 @@
     low[...] = jnp.zeros_like(low)
     mine = [slot_tile(z, s) for s in range(SLOTS)]
 
-    @pl.loop(0, 4)
+    @pl.loop(0, CHUNKS)
     def _(k):
-        rows = jnp.concatenate([wide(pool[mine[s] * 4 + k]) for s in range(SLOTS)], axis=0)
+        rows = jnp.concatenate([wide(pool[mine[s] * CHUNKS + k]) for s in range(SLOTS)], axis=0)
         r = jnp.dot(rows, matrix_rows(z, k), preferred_element_type=F32)
         for s in range(SLOTS):
             low[s] = low[s] + r[s * TILE:(s + 1) * TILE]
 
-    exchange(2, 5)
+    exchange(LAG, 9)
     for way in (0, 1):
         for sign in signs:
             copies[(1, way, sign)].wait_recv()
@@ -275,33 +277,39 @@
     for way in (0, 1):
         for sign in signs:
             forward(way, 0, sign)
-    exchange(5, 7)
+    exchange(9, 11)
     w_copy.wait()
     sib_copy.wait_recv()
     multiply(blk(0, 0), blk(1, 0))
-    exchange(7, 9)
+    exchange(11, 14)
     multiply(blk(0, 1), blk(0, -1))
-    exchange(9, 10)
-    for way in (0, 1):
-        for sign in signs:
-            copies[(2, way, sign)].wait_recv()
-        for sign in signs:
-            push((3, way, 2, sign), way, (2, 0), None, (0, sign))
-    for j in range(STEPS - LAG, STEPS):
-        for link in range(2):
-            z_copy(link, j).wait_recv()
-        use(j)
+    exchange(14, STEPS - 1)
+    for link in range(2):
+        z_copy(link, STEPS - 1 - LAG).wait_recv()
+    use(STEPS - 1 - LAG)
 
     for half in range(2):
         away_send[half] = away[half].astype(BF16)
     returns = [
         remote(away_send, away_recv.at[d - 1], f_send.at[d - 1], f_recv.at[d - 1], along(d)) for d in (2, 1, 3)
     ]
+    step(STEPS - 1, False)
+    for way in (0, 1):
+        for sign in signs:
+            copies[(2, way, sign)].wait_recv()
+        for sign in signs:
+            push((3, way, 2, sign), way, (2, 0), None, (0, sign))
     for o in signs:
         for way in (0, 1):
             for sign in signs:
                 forward(way, o, sign)
     multiply(blk(-1, 0), blk(1, 1))
+    for j in range(STEPS - LAG, STEPS):
+        for link in range(2):
+            z_copy(link, j).wait_recv()
+        use(j)
+        if j == STEPS - LAG:
+            multiply(blk(1, -1), blk(-1, 1))
     for copy in returns:
         copy.wait_recv()
     flags = table[base + 4 * STEPS + 1]
@@ -325,8 +333,8 @@
         low_full[pl.ds(t * TILE, TILE)] = jnp.where(keep, low[slot], 0.0).astype(BF16)
 
     b_copy.wait()
-    swaps = []
-    for q in range(N):
+
+    def delta(i, q):
         @pl.loop(0, N)
         def _(k):
             at_rows = pl.ds(pl.multiple_of((q * N + k) * 2 * COLS, 2 * COLS), 2 * COLS)
@@ -338,7 +346,7 @@
             d_send[q * N + k] = lax.select(c == 0, r[:, COLS:], r[:, :COLS])
 
         here = pl.ds(q * N, N)
-        swaps.append(remote(d_send.at[here], d_recv.at[here], s_send.at[1 + q], s_recv.at[1 + q], other))
+        return remote(d_send.at[here], d_recv.at[here], s_send.at[1 + i], s_recv.at[1 + i], other)
 
     def role(way, dx):
         q = (x + dx + N) % N
@@ -388,43 +396,47 @@
         (0, 2), (1, 2), (-1, 2), (2, 1), (2, -1), (2, 2),
     )
 
-    def point(p):
-        for turn in (3, 2, 1, 0):
-            i = p - 2 * turn
-            if 0 <= i < 8:
-                for block in order[2 * i:2 * i + 2]:
-                    for way in (1, 0):
-                        act(way, block, turn)
-
-    multiply(blk(1, -1), blk(-1, 1))
+    def stage(turn, blocks, ways=(1, 0)):
+        for block in blocks:
+            for way in ways:
+                act(way, block, turn)
+
+    early, late = order[:10], order[10:]
+    swaps = [delta(0, (z + 1) % N), delta(1, (z + N - 1) % N)]
+    stage(0, early[:8], (0,))
+    swaps[0].wait_recv()
+    stage(0, early[:8], (1,))
     for way in (0, 1):
         for sign in signs:
             copies[(4, way, 0, sign)].wait_recv()
     multiply(blk(-1, -1), blk(2, 0))
-    for copy in swaps:
+    stage(0, early[8:])
+    for way in (0, 1):
+        for sign in signs:
+            forward(way, 2, sign)
+    swaps.append(delta(2, (z + 2) % N))
+    swaps.append(delta(3, z))
+    for copy in swaps[1:]:
         copy.wait_recv()
-    point(0)
-    point(1)
-    for way in (0, 1):
-        for sign in signs:
-            forward(way, 2, sign)
-    point(2)
-    point(3)
-    point(4)
+    stage(1, early)
     for way in (0, 1):
         for o in signs:
             for sign in signs:
                 copies[(4, way, o, sign)].wait_recv()
     multiply(blk(0, 2), blk(1, 2))
-    point(5)
+    stage(0, late[:2])
     multiply(blk(-1, 2), blk(2, 1))
-    point(6)
+    stage(0, late[2:4])
+    stage(2, early)
     for way in (0, 1):
         for sign in signs:
             copies[(4, way, 2, sign)].wait_recv()
     multiply(blk(2, -1), blk(2, 2))
-    for p in range(7, 14):
-        point(p)
+    stage(0, late[4:])
+    stage(1, late)
+    stage(3, early)
+    stage(2, late)
+    stage(3, late)
     for block in order:
         @pl.when(role(1, block[0]) == 3)
         def _():
@@ -450,7 +462,7 @@
     anywhere = pl.BlockSpec(memory_space=pl.ANY)
     small = pl.BlockSpec(memory_space=pltpu.SMEM)
     tiles = hidden.reshape(TILES, TILE, UNITS)
-    matrix = down.reshape(4 * N, QUART, RANK)
+    matrix = down.reshape(N * CHUNKS, CHUNK, RANK)
     dma = pltpu.SemaphoreType.DMA
     return pl.pallas_call(
         kernel,
@@ -461,9 +473,9 @@
             pltpu.VMEM((N * N, UNITS, COLS), BF16),
             pltpu.VMEM((TILES, TILE, UNITS), BF16),
             pltpu.VMEM((TILES, TILE, UNITS), BF16),
-            pltpu.VMEM((48, QUART, COLS), BF16),
-            pltpu.VMEM((2, STEPS, QUART, COLS), BF16),
-            pltpu.VMEM((2, STEPS, QUART, COLS), BF16),
+            pltpu.VMEM((3 * N * CHUNKS, CHUNK, COLS), BF16),
+            pltpu.VMEM((2, STEPS, CHUNK, COLS), BF16),
+            pltpu.VMEM((2, STEPS, CHUNK, COLS), BF16),
             pltpu.VMEM((N * N * 2 * COLS, RANK), BF16),
             pltpu.VMEM((N * N, 2 * ROWS, COLS), BF16),
             pltpu.VMEM((N * N, ROWS, COLS), BF16),

time: 130 us -> 120 us (0.923); the launches traced: 128 us -> 120 us
  Pallas kernels: 125 us -> 117 us
    pallas_call x1, Pallas kernels: 125 us -> 117 us  [on_device(): pl.pallas_call(kernel, out_shape=jax.ShapeDtypeStruct((ROWS, N * 2 * COLS...]
where the time goes in v3:
time: 120 us
  Pallas kernels  117 us (98%)
  local copies, waits for them, and re-layouts  2.26 us (2%)
    pallas_call x1, Pallas kernels, on_device(): pl.pallas_call(kernel, out_shape=jax.ShapeDtypeStruct((ROWS, N * 2 * COLS...  117 us

profile of v3, /device:TPU:39, one launch (start us, length us, event | category | flops | bytes accessed | tf_op | source)
XLA Modules:
  0.0 119.8 jit_solution(12314402536232848044)
XLA Ops:
  0.0 117.5 %shard_map.73 = bf16[512,1024]{1,0:T(8,128)(2,1)} custom-call(s32[4]{0:T(128)} %bitcast.7, s32[4]{0:T(128)} %ranks.1, s32[1761]{0:T(1024)} %constant.2.clone.table, bf16[4,128,3584]{2,1,0:T(8,128)(2,1)} %bitcast.5, bf16[3584,128]{1,0:T(8,128)(2,1)} %w.1, bf16[28,512,256]{2,1,0:T(8,128)(2,1)} %bitcast.4, bf16[4096,256]{1,0:T(8,128)(2,1)} %bitcast.6), custom_call_target="tpu_custom_call" | custom-call | flops 20000000000 | bytes 15000000 | tf_op jit(solution)/shard_map/pallas_call | solution.py:467
  117.5 2.3 %copy.9 = bf16[512,1024]{1,0:T(8,128)(2,1)} copy(bf16[512,1024]{1,0:T(8,128)(2,1)} %shard_map.73) | data formatting | bytes 2097152

commit v4 on v3

--- a/solution.py
+++ b/solution.py
@@ -303,13 +303,12 @@
         for way in (0, 1):
             for sign in signs:
                 forward(way, o, sign)
-    multiply(blk(-1, 0), blk(1, 1))
     for j in range(STEPS - LAG, STEPS):
         for link in range(2):
             z_copy(link, j).wait_recv()
         use(j)
         if j == STEPS - LAG:
-            multiply(blk(1, -1), blk(-1, 1))
+            multiply(blk(-1, 0), blk(1, 1))
     for copy in returns:
         copy.wait_recv()
     flags = table[base + 4 * STEPS + 1]
@@ -335,7 +334,7 @@
     b_copy.wait()
 
     def delta(i, q):
-        @pl.loop(0, N)
+        @pl.loop(0, N, unroll=True)
         def _(k):
             at_rows = pl.ds(pl.multiple_of((q * N + k) * 2 * COLS, 2 * COLS), 2 * COLS)
             r = lax.dot_general(
@@ -393,7 +392,7 @@
 
     order = (
         (0, 0), (1, 0), (0, 1), (0, -1), (-1, 0), (1, 1), (1, -1), (-1, 1), (-1, -1), (2, 0),
-        (0, 2), (1, 2), (-1, 2), (2, 1), (2, -1), (2, 2),
+        (2, 1), (2, -1), (0, 2), (1, 2), (-1, 2), (2, 2),
     )
 
     def stage(turn, blocks, ways=(1, 0)):
@@ -403,9 +402,11 @@
 
     early, late = order[:10], order[10:]
     swaps = [delta(0, (z + 1) % N), delta(1, (z + N - 1) % N)]
-    stage(0, early[:8], (0,))
+    stage(0, early[:6], (0,))
     swaps[0].wait_recv()
-    stage(0, early[:8], (1,))
+    stage(0, early[:6], (1,))
+    multiply(blk(1, -1), blk(-1, 1))
+    stage(0, early[6:8])
     for way in (0, 1):
         for sign in signs:
             copies[(4, way, 0, sign)].wait_recv()
@@ -423,15 +424,15 @@
         for o in signs:
             for sign in signs:
                 copies[(4, way, o, sign)].wait_recv()
+    multiply(blk(2, 1), blk(2, -1))
+    stage(0, late[:2])
     multiply(blk(0, 2), blk(1, 2))
-    stage(0, late[:2])
-    multiply(blk(-1, 2), blk(2, 1))
     stage(0, late[2:4])
     stage(2, early)
     for way in (0, 1):
         for sign in signs:
             copies[(4, way, 2, sign)].wait_recv()
-    multiply(blk(2, -1), blk(2, 2))
+    multiply(blk(-1, 2), blk(2, 2))
     stage(0, late[4:])
     stage(1, late)
     stage(3, early)

time: 120 us -> 118 us (0.983)
    pallas_call x1, Pallas kernels: 117 us -> 116 us  [on_device(): pl.pallas_call(kernel, out_shape=jax.ShapeDtypeStruct((ROWS, N * 2 * COLS...]
where the time goes in v4:
time: 118 us
  Pallas kernels  116 us (98%)
  local copies, waits for them, and re-layouts  2.26 us (2%)
    pallas_call x1, Pallas kernels, on_device(): pl.pallas_call(kernel, out_shape=jax.ShapeDtypeStruct((ROWS, N * 2 * COLS...  116 us

profile of v4, /device:TPU:39, one launch (start us, length us, event | category | flops | bytes accessed | tf_op | source)
XLA Modules:
  0.0 118.3 jit_solution(16421480224175146088)
XLA Ops:
  0.0 116.0 %shard_map.73 = bf16[512,1024]{1,0:T(8,128)(2,1)} custom-call(s32[4]{0:T(128)} %bitcast.7, s32[4]{0:T(128)} %ranks.1, s32[1761]{0:T(1024)} %constant.2.clone.table, bf16[4,128,3584]{2,1,0:T(8,128)(2,1)} %bitcast.5, bf16[3584,128]{1,0:T(8,128)(2,1)} %w.1, bf16[28,512,256]{2,1,0:T(8,128)(2,1)} %bitcast.4, bf16[4096,256]{1,0:T(8,128)(2,1)} %bitcast.6), custom_call_target="tpu_custom_call" | custom-call | flops 20000000000 | bytes 15000000 | tf_op jit(solution)/shard_map/pallas_call | solution.py:468
  116.0 2.3 %copy.9 = bf16[512,1024]{1,0:T(8,128)(2,1)} copy(bf16[512,1024]{1,0:T(8,128)(2,1)} %shard_map.73) | data formatting | bytes 2097152
